TPU v7x, 32 devices: a whole 2x2x4 slice. The times are simulated.
32 devices in a mesh: gz: 2 (over x), gy: 16 (over z, y, core).
Axes of the slice: x: 2, y: 2, z: 4, core: 2. Of those that a mesh axis runs over, the one named last changes fastest.
Arguments:
- observed: float32 [64, 512, 768], P('gz', 'gy'), may hold values from 0.2 to 5
- estimate: float32 [64, 512, 768], P('gz', 'gy'), may hold values from 0.5 to 2
- taps_z: float32 [9], replicated, may hold values from 0.05 to 1
- taps_y: float32 [9], replicated, may hold values from 0.05 to 1
- taps_x: float32 [9], replicated, may hold values from 0.05 to 1
Outputs:
- updated: float32 [64, 512, 768], P('gz', 'gy')
- projection: float32 [512, 768], P('gy')
All inputs are finite; a program needn't handle non-finite values.
Results may differ from a plain program's by a relative error of at most 0.00002.
Values sent between devices are 32-bit elements; how exact they have to be, the bound alone decides.
A program may use at most 64 MiB of HBM per device.

v0:
```python
import jax
import jax.numpy as jnp
from jax import lax
from jax.sharding import PartitionSpec as P


def with_halo(shard, sides, width):
    for axis, dim in sides:
        peers, length = (lax.axis_size(axis), shard.shape[dim])
        up = [(i, (i + 1) % peers) for i in range(peers - 1)]
        down = [(j, i) for i, j in up]
        last = lax.slice_in_dim(shard, length - width, length, axis=dim)
        first = lax.slice_in_dim(shard, 0, width, axis=dim)
        before = lax.ppermute(last, axis, up)
        after = lax.ppermute(first, axis, down)
        shard = jnp.concatenate([before, shard, after], axis=dim)
    return shard


def valid_pass(padded, taps, axis):
    count = padded.shape[axis] - (taps.shape[0] - 1)
    total = taps[0] * lax.slice_in_dim(padded, 0, count, axis=axis)
    for index in range(1, taps.shape[0]):
        total = total + taps[index] * lax.slice_in_dim(padded, index, index + count, axis=axis)
    return total


def blur_along_x(volume, taps):
    radius = (taps.shape[0] - 1) // 2
    padded = jnp.pad(volume, ((0, 0), (0, 0), (radius, radius)))
    return valid_pass(padded, taps, 2)


def blur_padded(padded, taps_z, taps_y, taps_x):
    volume = valid_pass(padded, taps_z, 0)
    volume = valid_pass(volume, taps_y, 1)
    return blur_along_x(volume, taps_x)


def per_device(observed, estimate, taps_z, taps_y, taps_x):
    radius = (taps_z.shape[0] - 1) // 2
    back_z = taps_z[::-1]
    back_y = taps_y[::-1]
    back_x = taps_x[::-1]
    padded = with_halo(estimate, (("gz", 0), ("gy", 1)), radius)
    blurred = blur_padded(padded, taps_z, taps_y, taps_x)
    ratio = observed / blurred
    ratio_padded = with_halo(ratio, (("gz", 0), ("gy", 1)), radius)
    correction = blur_padded(ratio_padded, back_z, back_y, back_x)
    updated = estimate * correction
    local_max = jnp.max(updated, axis=0)
    projection = lax.pmax(local_max, "gz")
    return (updated, projection)


def solution(mesh):
    return jax.shard_map(
        per_device,
        mesh=mesh,
        in_specs=(P("gz", "gy", None), P("gz", "gy", None), P(), P(), P()),
        out_specs=(P("gz", "gy", None), P("gy", None)),
        check_vma=False,
    )
```

profile of v0, /device:TPU:20, one launch (start us, length us, event | category | flops | bytes accessed | tf_op | source)
XLA Modules:
  0.0 165.9 jit_solution(754237208460182436)
XLA Ops:
  7.2 0.0 all-reduce.4.cloned.1.call-start
  7.2 1.2 fusion.69
  8.4 3.4 %collective-permute-start = (f32[4,32,768]{2,1,0:T(8,128)S(1)}, f32[4,32,768]{2,1,0:T(8,128)S(1)}, u32[]{:S(2)}, u32[]{:S(2)}) collective-permute-start(f32[4,32,768]{2,1,0:T(8,128)S(1)} %get-tuple-element.14), channel_id=1, source_target_pairs={{0,16},{1,17},{2,18},{3,19},{4,20},{5,21},{6,22},{7,23},{8,24},{9,... | collective-permute-start | bytes 1179656 | tf_op jit(solution)/shard_map/ppermute | solution.py:14
  11.8 1.3 collective-permute-start.1
  13.1 3.7 %copy.21 = f32[32,32,768]{2,0,1:T(8,128)S(1)} copy(f32[32,32,768]{2,1,0:T(8,128)} %param.6) | data formatting | bytes 6291456 | tf_op args[1]
  16.8 0.0 copy-start.2
  16.9 0.0 copy-start.3
  16.9 0.0 copy-start.4
  16.9 3.3 %collective-permute-done = f32[4,32,768]{2,1,0:T(8,128)S(1)} collective-permute-done((f32[4,32,768]{2,1,0:T(8,128)S(1)}, f32[4,32,768]{2,1,0:T(8,128)S(1)}, u32[]{:S(2)}, u32[]{:S(2)}) %collective-permute-start) | collective-permute-done | bytes 393248 | tf_op jit(solution)/shard_map/ppermute | solution.py:14
  20.2 0.3 copy.13
  20.4 3.9 %collective-permute-done.1 = f32[4,32,768]{2,1,0:T(8,128)S(1)} collective-permute-done((f32[4,32,768]{2,1,0:T(8,128)S(1)}, f32[4,32,768]{2,1,0:T(8,128)S(1)}, u32[]{:S(2)}, u32[]{:S(2)}) %collective-permute-start.1) | collective-permute-done | bytes 393248 | tf_op jit(solution)/shard_map/ppermute | solution.py:15
  24.3 0.3 copy.15
  24.6 0.1 pad_maximum_fusion.7
  24.7 1.9 %collective-permute-start.2 = (f32[40,4,768]{2,0,1:T(8,128)S(1)}, f32[40,4,768]{2,0,1:T(8,128)S(1)}, u32[]{:S(2)}, u32[]{:S(2)}) collective-permute-start(f32[40,4,768]{2,0,1:T(8,128)S(1)} %get-tuple-element.10), channel_id=1, source_target_pairs={{0,1},{1,2},{2,3},{3,4},{4,5},{5,6},{6,7},{7,8},{8,9},{9,10},{10,1... | collective-permute-start | bytes 1474568 | tf_op jit(solution)/shard_map/ppermute | solution.py:14
  26.6 3.6 %collective-permute-start.3 = (f32[40,4,768]{2,0,1:T(8,128)S(1)}, f32[40,4,768]{2,0,1:T(8,128)S(1)}, u32[]{:S(2)}, u32[]{:S(2)}) collective-permute-start(f32[40,4,768]{2,0,1:T(8,128)S(1)} %get-tuple-element.11), channel_id=1, source_target_pairs={{1,0},{2,1},{3,2},{4,3},{5,4},{6,5},{7,6},{8,7},{9,8},{10,9},{11,1... | collective-permute-start | bytes 1474568 | tf_op jit(solution)/shard_map/ppermute | solution.py:15
  30.3 0.7 fusion.72
  30.9 0.7 fusion.71
  31.6 0.7 fusion.70
  32.3 7.8 %collective-permute-done.2 = f32[40,4,768]{2,0,1:T(8,128)S(1)} collective-permute-done((f32[40,4,768]{2,0,1:T(8,128)S(1)}, f32[40,4,768]{2,0,1:T(8,128)S(1)}, u32[]{:S(2)}, u32[]{:S(2)}) %collective-permute-start.2) | collective-permute-done | bytes 491552 | tf_op jit(solution)/shard_map/ppermute | solution.py:14
  40.1 0.0 collective-permute-done.3
  40.1 0.7 pad_maximum_fusion
  40.8 9.8 %fusion.8 = f32[32,40,768]{2,0,1:T(8,128)S(1)} fusion(f32[40,40,768]{2,0,1:T(8,128)S(1)} %pad_maximum_fusion, f32[]{:T(128)} %bitcast.12, f32[]{:T(128)} %bitcast.11, f32[]{:T(128)} %bitcast.10, f32[]{:T(128)} %bitcast.9, f32[]{:T(128)} %bitcast.8, f32[]{:T(128)} %bitcast.7, f32[]{:T(128)} %bitcast.6, f32[]{:T(128)} %bitcast.5, f32[]{:T(128)} %bitcast.2), kind=kLoop, calls=%fused_computation.36 | loop fusion | flops 16711680 | bytes 39321636 | tf_op jit(solution)/shard_map/add | solution.py:24
  50.6 0.0 copy-start.1
  50.6 9.0 %fusion.58 = f32[32,32,768]{2,0,1:T(8,128)S(1)} fusion(f32[32,40,768]{2,0,1:T(8,128)S(1)} %fusion.8, f32[]{:T(128)} %bitcast.19, f32[]{:T(128)} %bitcast.18, f32[]{:T(128)} %bitcast.17, f32[]{:T(128)} %bitcast.16, f32[]{:T(128)} %bitcast.15, f32[]{:T(128)} %bitcast.14, f32[]{:T(128)} %bitcast.13, f32[]{:T(128)} %bitcast.4, f32[]{:T(128)} %bitcast.1), kind=kLoop, calls=%fused_computation.104 | loop fusion | flops 13369344 | bytes 31457316 | tf_op jit(solution)/shard_map/add | solution.py:24
  59.6 12.6 %fusion.25 = f32[32,32,768]{2,0,1:T(8,128)S(1)} fusion(f32[32,32,768]{2,0,1:T(8,128)S(1)} %fusion.58, f32[32,32,768]{2,1,0:T(8,128)S(1)} %copy-done.1, f32[]{:T(128)} %bitcast.26, f32[]{:T(128)} %bitcast.25, f32[]{:T(128)} %bitcast.24, f32[]{:T(128)} %bitcast.23, f32[]{:T(128)} %bitcast.22, f32[]{:T(128)} %bitcast.21, f32[]{:T(128)} %bitcast.20, f32[]{:T(128)} %bitcast.3, ...), kind=kLoop, calls=%fused_computation.61 | loop fusion | flops 14155776 | bytes 9437220 | tf_op jit(solution)/shard_map/div | solution.py:47
  72.2 0.1 fusion.68
  72.4 0.1 copy.18
  72.5 1.3 collective-permute-start.5
  73.8 0.1 copy.17
  73.9 4.6 %collective-permute-start.4 = (f32[4,32,768]{2,1,0:T(8,128)S(1)}, f32[4,32,768]{2,1,0:T(8,128)S(1)}, u32[]{:S(2)}, u32[]{:S(2)}) collective-permute-start(f32[4,32,768]{2,1,0:T(8,128)S(1)} %copy.17), channel_id=1, source_target_pairs={{0,16},{1,17},{2,18},{3,19},{4,20},{5,21},{6,22},{7,23},{8,24},{9,... | collective-permute-start | bytes 1179656 | tf_op jit(solution)/shard_map/ppermute | solution.py:14
  78.5 6.2 %collective-permute-done.5 = f32[4,32,768]{2,1,0:T(8,128)S(1)} collective-permute-done((f32[4,32,768]{2,1,0:T(8,128)S(1)}, f32[4,32,768]{2,1,0:T(8,128)S(1)}, u32[]{:S(2)}, u32[]{:S(2)}) %collective-permute-start.5) | collective-permute-done | bytes 393248 | tf_op jit(solution)/shard_map/ppermute | solution.py:15
  84.7 0.3 copy.20
  84.9 1.0 collective-permute-done.4
  86.0 0.3 copy.19
  86.2 0.1 pad_maximum_fusion.4
  86.3 1.9 %collective-permute-start.6 = (f32[40,4,768]{2,0,1:T(8,128)S(1)}, f32[40,4,768]{2,0,1:T(8,128)S(1)}, u32[]{:S(2)}, u32[]{:S(2)}) collective-permute-start(f32[40,4,768]{2,0,1:T(8,128)S(1)} %get-tuple-element.8), channel_id=1, source_target_pairs={{0,1},{1,2},{2,3},{3,4},{4,5},{5,6},{6,7},{7,8},{8,9},{9,10},{10,1... | collective-permute-start | bytes 1474568 | tf_op jit(solution)/shard_map/ppermute | solution.py:14
  88.3 3.8 %collective-permute-start.7 = (f32[40,4,768]{2,0,1:T(8,128)S(1)}, f32[40,4,768]{2,0,1:T(8,128)S(1)}, u32[]{:S(2)}, u32[]{:S(2)}) collective-permute-start(f32[40,4,768]{2,0,1:T(8,128)S(1)} %get-tuple-element.9), channel_id=1, source_target_pairs={{1,0},{2,1},{3,2},{4,3},{5,4},{6,5},{7,6},{8,7},{9,8},{10,9},{11,1... | collective-permute-start | bytes 1474568 | tf_op jit(solution)/shard_map/ppermute | solution.py:15
  92.1 9.7 %collective-permute-done.6 = f32[40,4,768]{2,0,1:T(8,128)S(1)} collective-permute-done((f32[40,4,768]{2,0,1:T(8,128)S(1)}, f32[40,4,768]{2,0,1:T(8,128)S(1)}, u32[]{:S(2)}, u32[]{:S(2)}) %collective-permute-start.6) | collective-permute-done | bytes 491552 | tf_op jit(solution)/shard_map/ppermute | solution.py:14
  101.8 0.0 collective-permute-done.7
  101.8 0.7 pad_maximum_fusion.1
  102.5 9.8 %fusion = f32[32,40,768]{2,0,1:T(8,128)S(1)} fusion(f32[40,40,768]{2,0,1:T(8,128)S(1)} %pad_maximum_fusion.1, f32[]{:T(128)} %bitcast.12, f32[]{:T(128)} %bitcast.11, f32[]{:T(128)} %bitcast.10, f32[]{:T(128)} %bitcast.9, f32[]{:T(128)} %bitcast.8, f32[]{:T(128)} %bitcast.7, f32[]{:T(128)} %bitcast.6, f32[]{:T(128)} %bitcast.5, f32[]{:T(128)} %bitcast.2), kind=kLoop, calls=%fused_computation.19 | loop fusion | flops 16711680 | bytes 39321636 | tf_op jit(solution)/shard_map/add | solution.py:24
  112.3 0.0 copy-start
  112.3 9.0 %fusion.50 = f32[32,32,768]{2,0,1:T(8,128)S(1)} fusion(f32[32,40,768]{2,0,1:T(8,128)S(1)} %fusion, f32[]{:T(128)} %bitcast.19, f32[]{:T(128)} %bitcast.18, f32[]{:T(128)} %bitcast.17, f32[]{:T(128)} %bitcast.16, f32[]{:T(128)} %bitcast.15, f32[]{:T(128)} %bitcast.14, f32[]{:T(128)} %bitcast.13, f32[]{:T(128)} %bitcast.4, f32[]{:T(128)} %bitcast.1), kind=kLoop, calls=%fused_computation.87 | loop fusion | flops 13369344 | bytes 31457316 | tf_op jit(solution)/shard_map/add | solution.py:24
  121.3 13.9 %fusion.66 = (f32[32,768]{1,0:T(8,128)}, f32[32,32,768]{2,0,1:T(8,128)S(1)}) fusion(f32[]{:T(128)} %bitcast.3, f32[]{:T(128)} %bitcast.20, f32[]{:T(128)} %bitcast.21, f32[]{:T(128)} %bitcast.22, f32[32,32,768]{2,0,1:T(8,128)S(1)} %fusion.50, f32[]{:T(128)} %bitcast.23, f32[]{:T(128)} %bitcast.24, f32[]{:T(128)} %bitcast.25, f32[]{:T(128)} %bitcast.26, ...), kind=kLoop, calls=%fused_computation.126 | loop fusion | flops 14917632 | bytes 9535524 | tf_op jit(solution)/shard_map/reduce_max | solution.py:51
  135.2 0.0 all-reduce.4.cloned.1.call-update
  135.3 3.5 %copy.22 = f32[32,32,768]{2,1,0:T(8,128)} copy(f32[32,32,768]{2,0,1:T(8,128)S(1)} %get-tuple-element.7) | data formatting | bytes 6291456
  138.7 18.7 %all-reduce.4.cloned.1.call-done = f32[32,768]{1,0:T(8,128)} async-done(((f32[32,768]{1,0:T(8,128)}), f32[32,768]{1,0:T(8,128)}) %all-reduce.4.cloned.1.call-update) | async-done | bytes 98320 | tf_op jit(solution)/shard_map/pmax | solution.py:52
  157.5 1.5 copy.27
  (5 shorter events, 0.0 us)
Async XLA Ops:
  7.2 150.3 %all-reduce.4.cloned.1.call-start = ((), (), s32[]{:S(2)}) async-start(), calls=%async_computation | async-start | bytes 196608 | tf_op jit(solution)/shard_map/pmax | solution.py:52
  8.4 11.8 %collective-permute-start = (f32[4,32,768]{2,1,0:T(8,128)S(1)}, f32[4,32,768]{2,1,0:T(8,128)S(1)}, u32[]{:S(2)}, u32[]{:S(2)}) collective-permute-start(f32[4,32,768]{2,1,0:T(8,128)S(1)} %get-tuple-element.14), channel_id=1, source_target_pairs={{0,16},{1,17},{2,18},{3,19},{4,20},{5,21},{6,22},{7,23},{8,24},{9,... | collective-permute-start | bytes 1179656 | tf_op jit(solution)/shard_map/ppermute | solution.py:14
  11.8 12.5 %collective-permute-start.1 = (f32[4,32,768]{2,1,0:T(8,128)S(1)}, f32[4,32,768]{2,1,0:T(8,128)S(1)}, u32[]{:S(2)}, u32[]{:S(2)}) collective-permute-start(f32[4,32,768]{2,1,0:T(8,128)S(1)} %get-tuple-element.15), channel_id=1, source_target_pairs={{16,0},{17,1},{18,2},{19,3},{20,4},{21,5},{22,6},{23,7},{24,8},{25... | collective-permute-start | bytes 1179656 | tf_op jit(solution)/shard_map/ppermute | solution.py:15
  16.8 13.4 %copy-start.2 = (f32[9]{0:T(128)S(1)}, f32[9]{0:T(128)}, u32[]{:S(2)}) copy-start(f32[9]{0:T(128)} %param.7) | copy-start | bytes 112
  16.9 14.1 %copy-start.3 = (f32[9]{0:T(128)S(1)}, f32[9]{0:T(128)}, u32[]{:S(2)}) copy-start(f32[9]{0:T(128)} %param.8) | copy-start | bytes 112
  16.9 14.8 %copy-start.4 = (f32[9]{0:T(128)S(1)}, f32[9]{0:T(128)}, u32[]{:S(2)}) copy-start(f32[9]{0:T(128)} %param.9) | copy-start | bytes 112
  24.7 15.4 %collective-permute-start.2 = (f32[40,4,768]{2,0,1:T(8,128)S(1)}, f32[40,4,768]{2,0,1:T(8,128)S(1)}, u32[]{:S(2)}, u32[]{:S(2)}) collective-permute-start(f32[40,4,768]{2,0,1:T(8,128)S(1)} %get-tuple-element.10), channel_id=1, source_target_pairs={{0,1},{1,2},{2,3},{3,4},{4,5},{5,6},{6,7},{7,8},{8,9},{9,10},{10,1... | collective-permute-start | bytes 1474568 | tf_op jit(solution)/shard_map/ppermute | solution.py:14
  26.6 13.5 %collective-permute-start.3 = (f32[40,4,768]{2,0,1:T(8,128)S(1)}, f32[40,4,768]{2,0,1:T(8,128)S(1)}, u32[]{:S(2)}, u32[]{:S(2)}) collective-permute-start(f32[40,4,768]{2,0,1:T(8,128)S(1)} %get-tuple-element.11), channel_id=1, source_target_pairs={{1,0},{2,1},{3,2},{4,3},{5,4},{6,5},{7,6},{8,7},{9,8},{10,9},{11,1... | collective-permute-start | bytes 1474568 | tf_op jit(solution)/shard_map/ppermute | solution.py:15
  50.6 9.0 %copy-start.1 = (f32[32,32,768]{2,1,0:T(8,128)S(1)}, f32[32,32,768]{2,1,0:T(8,128)}, u32[]{:S(2)}) copy-start(f32[32,32,768]{2,1,0:T(8,128)} %param.5) | copy-start | bytes 9437188
  72.5 12.2 %collective-permute-start.5 = (f32[4,32,768]{2,1,0:T(8,128)S(1)}, f32[4,32,768]{2,1,0:T(8,128)S(1)}, u32[]{:S(2)}, u32[]{:S(2)}) collective-permute-start(f32[4,32,768]{2,1,0:T(8,128)S(1)} %copy.18), channel_id=1, source_target_pairs={{16,0},{17,1},{18,2},{19,3},{20,4},{21,5},{22,6},{23,7},{24,8},{25... | collective-permute-start | bytes 1179656 | tf_op jit(solution)/shard_map/ppermute | solution.py:15
  73.9 12.1 %collective-permute-start.4 = (f32[4,32,768]{2,1,0:T(8,128)S(1)}, f32[4,32,768]{2,1,0:T(8,128)S(1)}, u32[]{:S(2)}, u32[]{:S(2)}) collective-permute-start(f32[4,32,768]{2,1,0:T(8,128)S(1)} %copy.17), channel_id=1, source_target_pairs={{0,16},{1,17},{2,18},{3,19},{4,20},{5,21},{6,22},{7,23},{8,24},{9,... | collective-permute-start | bytes 1179656 | tf_op jit(solution)/shard_map/ppermute | solution.py:14
  86.3 15.4 %collective-permute-start.6 = (f32[40,4,768]{2,0,1:T(8,128)S(1)}, f32[40,4,768]{2,0,1:T(8,128)S(1)}, u32[]{:S(2)}, u32[]{:S(2)}) collective-permute-start(f32[40,4,768]{2,0,1:T(8,128)S(1)} %get-tuple-element.8), channel_id=1, source_target_pairs={{0,1},{1,2},{2,3},{3,4},{4,5},{5,6},{6,7},{7,8},{8,9},{9,10},{10,1... | collective-permute-start | bytes 1474568 | tf_op jit(solution)/shard_map/ppermute | solution.py:14
  88.3 13.5 %collective-permute-start.7 = (f32[40,4,768]{2,0,1:T(8,128)S(1)}, f32[40,4,768]{2,0,1:T(8,128)S(1)}, u32[]{:S(2)}, u32[]{:S(2)}) collective-permute-start(f32[40,4,768]{2,0,1:T(8,128)S(1)} %get-tuple-element.9), channel_id=1, source_target_pairs={{1,0},{2,1},{3,2},{4,3},{5,4},{6,5},{7,6},{8,7},{9,8},{10,9},{11,1... | collective-permute-start | bytes 1474568 | tf_op jit(solution)/shard_map/ppermute | solution.py:15
  112.3 9.0 %copy-start = (f32[32,32,768]{2,1,0:T(8,128)S(1)}, f32[32,32,768]{2,1,0:T(8,128)}, u32[]{:S(2)}) copy-start(f32[32,32,768]{2,1,0:T(8,128)} %param.6) | copy-start | bytes 9437188
Sparse Core Ops, SparseCore 0:
  135.4 22.0 all-reduce.3
where the time goes:
time: 168 us; the launch traced here: 166 us
  other arithmetic  65.7 us (39%)
  waiting for transfers between devices  50.6 us (30%)
  starting transfers between devices  21.9 us (13%)
  between operations  14.3 us (9%)
  local copies, waits for them, and re-layouts  13.3 us (8%)
    add x4, other arithmetic, valid_pass(): total + taps[index] * lax.slice_in_dim(padded, index, index + count, axis...  37.5 us
    ppermute x4, waiting for transfers between devices, with_halo(): before = lax.ppermute(last, axis, up)  21.7 us
    pmax x1, waiting for transfers between devices, per_device(): projection = lax.pmax(local_max, 'gz')  18.7 us
    reduce_max x1, other arithmetic, per_device(): local_max = jnp.max(updated, axis=0)  13.9 us
    div x1, other arithmetic, per_device(): ratio = observed / blurred  12.6 us
    ppermute x4, starting transfers between devices, with_halo(): before = lax.ppermute(last, axis, up)  11.9 us
    ppermute x4, waiting for transfers between devices, with_halo(): after = lax.ppermute(first, axis, down)  10.1 us
    ppermute x4, starting transfers between devices, with_halo(): after = lax.ppermute(first, axis, down)  10 us
  transfers between devices with their start and end apart: 9, of which 7 were waited for; matrix products, arithmetic and copies ran while one was open for 6% of the time, Pallas kernels for 0%

commit v1 on v0

v1 whole, which is shorter than its diff:
```python
import functools

import jax
import jax.numpy as jnp
from jax import lax
from jax.experimental import pallas as pl
from jax.experimental.pallas import tpu as pltpu
from jax.sharding import PartitionSpec as P

F32 = jnp.float32
BF16 = jnp.bfloat16
MESH = pl.DeviceIdType.MESH
DIRS = tuple((dz, dy) for dz in (-1, 0, 1) for dy in (-1, 0, 1) if (dz, dy) != (0, 0))


def split(v):
    hi = v.astype(BF16)
    lo = (v - hi.astype(F32)).astype(BF16)
    return hi, lo


def kernel(nz, ny, obs_hbm, est_hbm, wz_ref, wy_ref, wx_ref, out_ref, proj_ref,
           est_pad, rat_pad, mid, obs, band_x, band_y, mx_all,
           e_send, e_recv, r_send, r_recv, p_send, p_recv, l_sem):
    taps = wz_ref.shape[0]
    rad = (taps - 1) // 2
    Z, Y, X = obs.shape
    OFF = 8
    gz, gy = lax.axis_index("gz"), lax.axis_index("gy")

    def valid(dz, dy):
        z, y = gz + dz, gy + dy
        return (z >= 0) & (z < nz) & (y >= 0) & (y < ny)

    load_est = pltpu.make_async_copy(
        est_hbm, est_pad.at[pl.ds(rad, Z), pl.ds(OFF, Y), :], l_sem.at[0])
    load_obs = pltpu.make_async_copy(obs_hbm, obs, l_sem.at[1])
    load_est.start()
    load_obs.start()

    barrier = pltpu.get_barrier_semaphore()
    for buf in (est_pad, rat_pad):
        buf[:, 0:OFF, :] = jnp.zeros((Z + 2 * rad, OFF, X), F32)
        buf[:, OFF + Y:, :] = jnp.zeros((Z + 2 * rad, OFF, X), F32)

        @pl.when(gz == 0)
        def _():
            buf[0:rad, OFF:OFF + Y, :] = jnp.zeros((rad, Y, X), F32)

        @pl.when(gz == nz - 1)
        def _():
            buf[rad + Z:, OFF:OFF + Y, :] = jnp.zeros((rad, Y, X), F32)

    count = jnp.int32(nz - 1)
    for dz, dy in DIRS:
        ok = valid(dz, dy)
        count = count + ok.astype(jnp.int32)

        @pl.when(ok)
        def _():
            pl.semaphore_signal(barrier, inc=1, device_id=(gz + dz, gy + dy), device_id_type=MESH)
    for d in range(1, nz):
        pl.semaphore_signal(barrier, inc=1, device_id=(lax.rem(gz + d, nz), gy), device_id_type=MESH)
    pl.semaphore_wait(barrier, count)

    def span(d, n, width):
        if d == 0:
            return pl.ds(0, n), pl.ds(0, n)
        if d > 0:
            return pl.ds(n - width, width), pl.ds(-width, width)
        return pl.ds(0, width), pl.ds(n, width)

    def shifted(s, off):
        return pl.ds(s.start + off, s.size)

    def halo(src, zo, yo, pad, send, recv):
        copies = []
        for i, (dz, dy) in enumerate(DIRS):
            sz, tz = span(dz, Z, rad)
            sy, ty = span(dy, Y, rad)
            copies.append((dz, dy, pltpu.make_async_remote_copy(
                src_ref=src.at[shifted(sz, zo), shifted(sy, yo), :],
                dst_ref=pad.at[shifted(tz, rad), shifted(ty, OFF), :],
                send_sem=send.at[i], recv_sem=recv.at[i],
                device_id=(gz + dz, gy + dy), device_id_type=MESH)))
        return copies

    def start(copies):
        for dz, dy, c in copies:
            @pl.when(valid(dz, dy))
            def _():
                c.start()

    def wait_recv(copies):
        for dz, dy, c in copies:
            @pl.when(valid(-dz, -dy))
            def _():
                c.wait_recv()

    def wait_send(copies):
        for dz, dy, c in copies:
            @pl.when(valid(dz, dy))
            def _():
                c.wait_send()

    e_copies = halo(est_hbm, 0, 0, est_pad, e_send, e_recv)
    start(e_copies)

    def band(shape, off, w_ref, back):
        diff = lax.broadcasted_iota(jnp.int32, shape, 0) - lax.broadcasted_iota(jnp.int32, shape, 1)
        total = jnp.zeros(shape, F32)
        for k in range(taps):
            w = w_ref[taps - 1 - k] if back else w_ref[k]
            total = jnp.where(diff == off + k, w, total)
        return total

    for b in range(2):
        hi, lo = split(band((512, 256), 128 - rad, wx_ref, b))
        band_x[b, 0] = hi
        band_x[b, 1] = lo
        diff = (lax.broadcasted_iota(jnp.int32, (Y, Y + 2 * OFF), 1)
                - lax.broadcasted_iota(jnp.int32, (Y, Y + 2 * OFF), 0))
        total = jnp.zeros(diff.shape, F32)
        for k in range(taps):
            w = wy_ref[taps - 1 - k] if b else wy_ref[k]
            total = jnp.where(diff == OFF - rad + k, w, total)
        hi, lo = split(total)
        band_y[b] = jnp.concatenate([hi, hi, lo], axis=1)

    def z_pass(pad, back):
        ws = [wz_ref[taps - 1 - k] if back else wz_ref[k] for k in range(taps)]
        nc = X // 128

        def body(i, _):
            r = pl.ds(pl.multiple_of((i // nc) * 8, 8), 8)
            c = pl.ds(pl.multiple_of(lax.rem(i, nc) * 128, 128), 128)
            vals = [pad[p, r, c] for p in range(Z + taps - 1)]
            for z in range(Z):
                t = ws[0] * vals[z]
                for k in range(1, taps):
                    t = t + ws[k] * vals[z + k]
                mid[z, r, c] = t
            return 0

        lax.fori_loop(0, (Y // 8 + 2) * nc, body, 0)

    G = 4
    NT = 256

    def yx_pass(back, use):
        def body(g, carry):
            rows = []
            for j in range(G):
                hi, lo = split(mid[g * G + j])
                rhs = jnp.concatenate([hi, lo, hi], axis=0)
                rows.append(jnp.dot(band_y[back], rhs, preferred_element_type=F32))
            hi, lo = split(jnp.concatenate(rows, axis=0))
            for n in range(X // NT):
                k0, k1 = max(n * NT - 128, 0), min(n * NT + NT + 128, X)
                b0 = k0 - (n * NT - 128)
                th = band_x[back, 0, b0:b0 + k1 - k0, :]
                tl = band_x[back, 1, b0:b0 + k1 - k0, :]
                h, l = hi[:, k0:k1], lo[:, k0:k1]
                t = (jnp.dot(h, th, preferred_element_type=F32)
                     + jnp.dot(l, th, preferred_element_type=F32)
                     + jnp.dot(h, tl, preferred_element_type=F32))
                use(g, pl.ds(n * NT, NT), t.reshape(G, Y, NT))
            return carry

        lax.fori_loop(0, Z // G, body, 0)

    load_est.wait()
    wait_recv(e_copies)
    z_pass(est_pad, 0)
    load_obs.wait()

    def use_ratio(g, c, t):
        rat_pad[pl.ds(rad + g * G, G), OFF:OFF + Y, c] = obs[pl.ds(g * G, G), :, c] / t

    yx_pass(0, use_ratio)

    r_copies = halo(rat_pad, rad, OFF, rat_pad, r_send, r_recv)
    start(r_copies)
    wait_recv(r_copies)
    z_pass(rat_pad, 1)

    mx_all[0] = jnp.full((Y, X), -jnp.inf, F32)

    def use_corr(g, c, t):
        u = est_pad[pl.ds(rad + g * G, G), OFF:OFF + Y, c] * t
        out_ref[pl.ds(g * G, G), :, c] = u
        mx_all[0, :, c] = jnp.maximum(mx_all[0, :, c], jnp.max(u, axis=0))

    yx_pass(1, use_corr)

    p_copies = []
    for d in range(1, nz):
        c = pltpu.make_async_remote_copy(
            src_ref=mx_all.at[0], dst_ref=mx_all.at[d],
            send_sem=p_send.at[d - 1], recv_sem=p_recv.at[d - 1],
            device_id=(lax.rem(gz + d, nz), gy), device_id_type=MESH)
        c.start()
        p_copies.append(c)
    best = mx_all[0]
    for d, c in enumerate(p_copies):
        c.wait_recv()
        best = jnp.maximum(best, mx_all[d + 1])
    proj_ref[...] = best
    wait_send(e_copies)
    wait_send(r_copies)
    for c in p_copies:
        c.wait_send()


def per_device(nz, ny, observed, estimate, taps_z, taps_y, taps_x):
    Z, Y, X = observed.shape
    taps = taps_z.shape[0]
    rad = (taps - 1) // 2
    pad = (Z + 2 * rad, Y + 16, X)
    nd = len(DIRS)
    smem = pl.BlockSpec(memory_space=pltpu.SMEM)
    hbm = pl.BlockSpec(memory_space=pl.ANY)
    vmem = pl.BlockSpec(memory_space=pltpu.VMEM)
    dma = pltpu.SemaphoreType.DMA
    return pl.pallas_call(
        functools.partial(kernel, nz, ny),
        out_shape=(jax.ShapeDtypeStruct((Z, Y, X), F32), jax.ShapeDtypeStruct((Y, X), F32)),
        in_specs=[hbm, hbm, smem, smem, smem],
        out_specs=(vmem, vmem),
        scratch_shapes=[
            pltpu.VMEM(pad, F32),
            pltpu.VMEM(pad, F32),
            pltpu.VMEM((Z, Y + 16, X), F32),
            pltpu.VMEM((Z, Y, X), F32),
            pltpu.VMEM((2, 2, 512, 256), BF16),
            pltpu.VMEM((2, Y, 3 * (Y + 16)), BF16),
            pltpu.VMEM((nz, Y, X), F32),
            dma((nd,)), dma((nd,)), dma((nd,)), dma((nd,)),
            dma((nz - 1,)), dma((nz - 1,)), dma((2,)),
        ],
        compiler_params=pltpu.CompilerParams(
            collective_id=0, has_side_effects=True, vmem_limit_bytes=50 * 1024 * 1024),
        name="deconvolve",
    )(observed, estimate, taps_z, taps_y, taps_x)


def solution(mesh):
    return jax.shard_map(
        functools.partial(per_device, mesh.shape["gz"], mesh.shape["gy"]),
        mesh=mesh,
        in_specs=(P("gz", "gy", None), P("gz", "gy", None), P(), P(), P()),
        out_specs=(P("gz", "gy", None), P("gy", None)),
        check_vma=False,
    )
```

time: 168 us -> 54.4 us (0.32); the launches traced: 166 us -> 54.3 us
  other arithmetic: 65.7 us -> 0 us
  waiting for transfers between devices: 50.6 us -> 0 us
  Pallas kernels: 0 us -> 49.4 us
  starting transfers between devices: 21.9 us -> 0 us
  between operations: 14.3 us -> 0.65 us
  local copies, waits for them, and re-layouts: 13.3 us -> 4.26 us
    pallas_call x0 -> x1, Pallas kernels: none -> 49.4 us  [per_device(): pl.pallas_call(functools.partial(kernel, nz, ny), out_shape=(jax.ShapeDty...]
    add x4 -> x0, other arithmetic: 37.5 us -> none  [valid_pass(): total + taps[index] * lax.slice_in_dim(padded, index, index + count, axis...]
    ppermute x8 -> x0, waiting for transfers between devices: 31.8 us -> none  [the longest x4 21.7 us: with_halo(): before = lax.ppermute(last, axis, up)]
    ppermute x8 -> x0, starting transfers between devices: 21.9 us -> none  [the longest x4 11.9 us: with_halo(): before = lax.ppermute(last, axis, up)]
    pmax x1 -> x0, waiting for transfers between devices: 18.7 us -> none  [per_device(): projection = lax.pmax(local_max, 'gz')]
    reduce_max x1 -> x0, other arithmetic: 13.9 us -> none  [per_device(): local_max = jnp.max(updated, axis=0)]
    div x1 -> x0, other arithmetic: 12.6 us -> none  [per_device(): ratio = observed / blurred]
    unnamed x13 -> x8, local copies, waits for them, and re-layouts: 8.77 us -> 4.26 us
  transfers between devices with their start and end apart: 9 -> 0, of which waited for: 7 -> 0; matrix products, arithmetic and copies ran while one was open for 6% -> 0% of each run, Pallas kernels for 0% -> 0%
where the time goes in v1:
time: 54.4 us; the launch traced here: 54.3 us
  Pallas kernels  49.4 us (91%)
  local copies, waits for them, and re-layouts  4.26 us (8%)
  between operations  0.65 us (1%)
    pallas_call x1, Pallas kernels, per_device(): pl.pallas_call(functools.partial(kernel, nz, ny), out_shape=(jax.ShapeDty...  49.4 us
    unnamed x8, local copies, waits for them, and re-layouts  4.26 us

profile of v1, /device:TPU:20, one launch (start us, length us, event | category | flops | bytes accessed | tf_op | source)
XLA Modules:
  0.0 54.3 jit_solution(13467547316595011676)
XLA Ops:
  0.6 0.0 copy-start
  0.6 0.6 %copy-done = f32[9]{0:T(128)S(1)} copy-done((f32[9]{0:T(128)S(1)}, f32[9]{0:T(128)}, u32[]{:S(2)}) %copy-start) | copy-done | bytes 60
  1.3 0.0 copy-start.1
  1.3 0.7 %copy-done.1 = f32[9]{0:T(128)S(1)} copy-done((f32[9]{0:T(128)S(1)}, f32[9]{0:T(128)}, u32[]{:S(2)}) %copy-start.1) | copy-done | bytes 60
  1.9 0.0 copy-start.2
  1.9 0.7 %copy-done.2 = f32[9]{0:T(128)S(1)} copy-done((f32[9]{0:T(128)S(1)}, f32[9]{0:T(128)}, u32[]{:S(2)}) %copy-start.2) | copy-done | bytes 60
  2.6 49.4 %deconvolve.1 = (f32[32,32,768]{2,1,0:T(8,128)S(1)}, f32[32,768]{1,0:T(8,128)S(1)}) custom-call(f32[32,32,768]{2,1,0:T(8,128)} %obs_hbm.1, f32[32,32,768]{2,1,0:T(8,128)} %est_hbm.1, f32[9]{0:T(128)S(1)} %copy-done, f32[9]{0:T(128)S(1)} %copy-done.1, f32[9]{0:T(128)S(1)} %copy-done.2), custom_call_target="tpu_custom_call" | custom-call | tf_op jit(solution)/shard_map/deconvolve/pallas_call | solution.py:225
  52.0 1.7 %copy.9 = f32[32,32,768]{2,1,0:T(8,128)} copy(f32[32,32,768]{2,1,0:T(8,128)S(1)} %get-tuple-element.4) | data formatting | bytes 6291456
  53.6 0.6 %copy.10 = f32[32,768]{1,0:T(8,128)} copy(f32[32,768]{1,0:T(8,128)S(1)} %get-tuple-element.5) | data formatting | bytes 196608
Async XLA Ops:
  0.6 0.7 %copy-start = (f32[9]{0:T(128)S(1)}, f32[9]{0:T(128)}, u32[]{:S(2)}) copy-start(f32[9]{0:T(128)} %wz_ref.1) | copy-start | bytes 112
  1.3 0.7 %copy-start.1 = (f32[9]{0:T(128)S(1)}, f32[9]{0:T(128)}, u32[]{:S(2)}) copy-start(f32[9]{0:T(128)} %wy_ref.1) | copy-start | bytes 112
  1.9 0.7 %copy-start.2 = (f32[9]{0:T(128)S(1)}, f32[9]{0:T(128)}, u32[]{:S(2)}) copy-start(f32[9]{0:T(128)} %wx_ref.1) | copy-start | bytes 112

commit v2 on v1

v2 whole, which is shorter than its diff:
```python
import functools

import jax
import jax.numpy as jnp
from jax import lax
from jax.experimental import pallas as pl
from jax.experimental.pallas import tpu as pltpu
from jax.sharding import PartitionSpec as P

F32 = jnp.float32
BF16 = jnp.bfloat16
MESH = pl.DeviceIdType.MESH
DIRS = tuple((dz, dy) for dz in (-1, 0, 1) for dy in (-1, 0, 1) if (dz, dy) != (0, 0))


def split(v):
    hi = v.astype(BF16)
    lo = (v - hi.astype(F32)).astype(BF16)
    return hi, lo


def kernel(nz, ny, cw, obs_hbm, est_hbm, wz_hbm, wy_hbm, wx_hbm, out, proj_ref,
           est_pad, rat_pad, mid, yh, yl, obs, band_x, band_y, mx_all, w_ref,
           e_send, e_recv, r_send, r_recv, p_send, p_recv, l_sem, w_sem):
    taps = w_ref.shape[1]
    rad = (taps - 1) // 2
    Z, Y, X = obs.shape
    OFF = 8
    NC = X // cw
    gz, gy = lax.axis_index("gz"), lax.axis_index("gy")

    def valid(dz, dy):
        z, y = gz + dz, gy + dy
        return (z >= 0) & (z < nz) & (y >= 0) & (y < ny)

    def cols(c):
        return pl.ds(c * cw, cw)

    w_loads = [pltpu.make_async_copy(w, w_ref.at[i], w_sem.at[i])
               for i, w in enumerate((wz_hbm, wy_hbm, wx_hbm))]
    for c in w_loads:
        c.start()
    est_loads, obs_loads = [], []
    for c in range(NC):
        est_loads.append(pltpu.make_async_copy(
            est_hbm.at[:, :, cols(c)], est_pad.at[pl.ds(rad, Z), pl.ds(OFF, Y), cols(c)],
            l_sem.at[c]))
        obs_loads.append(pltpu.make_async_copy(
            obs_hbm.at[:, :, cols(c)], obs.at[:, :, cols(c)], l_sem.at[NC + c]))

    barrier = pltpu.get_barrier_semaphore()
    for buf in (est_pad, rat_pad):
        buf[:, 0:OFF, :] = jnp.zeros((Z + 2 * rad, OFF, X), F32)
        buf[:, OFF + Y:, :] = jnp.zeros((Z + 2 * rad, OFF, X), F32)

        @pl.when(gz == 0)
        def _():
            buf[0:rad, OFF:OFF + Y, :] = jnp.zeros((rad, Y, X), F32)

        @pl.when(gz == nz - 1)
        def _():
            buf[rad + Z:, OFF:OFF + Y, :] = jnp.zeros((rad, Y, X), F32)

    count = jnp.int32(nz - 1)
    for dz, dy in DIRS:
        ok = valid(dz, dy)
        count = count + ok.astype(jnp.int32)

        @pl.when(ok)
        def _():
            pl.semaphore_signal(barrier, inc=1, device_id=(gz + dz, gy + dy), device_id_type=MESH)
    for d in range(1, nz):
        pl.semaphore_signal(barrier, inc=1, device_id=(lax.rem(gz + d, nz), gy), device_id_type=MESH)
    pl.semaphore_wait(barrier, count)

    def span(d, n, width):
        if d == 0:
            return (0, n), (0, n)
        if d > 0:
            return (n - width, width), (-width, width)
        return (0, width), (n, width)

    def shifted(s, off):
        return pl.ds(s[0] + off, s[1])

    def halo(c, src, zo, yo, pad, send, recv):
        copies = []
        for i, (dz, dy) in enumerate(DIRS):
            sz, tz = span(dz, Z, rad)
            sy, ty = span(dy, Y, rad)
            copies.append((dz, dy, pltpu.make_async_remote_copy(
                src_ref=src.at[shifted(sz, zo), shifted(sy, yo), cols(c)],
                dst_ref=pad.at[shifted(tz, rad), shifted(ty, OFF), cols(c)],
                send_sem=send.at[c * len(DIRS) + i], recv_sem=recv.at[c * len(DIRS) + i],
                device_id=(gz + dz, gy + dy), device_id_type=MESH)))
        return copies

    def start(copies):
        for dz, dy, c in copies:
            @pl.when(valid(dz, dy))
            def _():
                c.start()

    def wait_recv(copies):
        for dz, dy, c in copies:
            @pl.when(valid(-dz, -dy))
            def _():
                c.wait_recv()

    def wait_send(copies):
        for dz, dy, c in copies:
            @pl.when(valid(dz, dy))
            def _():
                c.wait_send()

    e_copies = [halo(c, est_hbm, 0, 0, est_pad, e_send, e_recv) for c in range(NC)]
    r_copies = [halo(c, rat_pad, rad, OFF, rat_pad, r_send, r_recv) for c in range(NC)]
    start(e_copies[0])
    for c in range(NC):
        est_loads[c].start()
    for c in range(NC):
        obs_loads[c].start()

    for c in w_loads:
        c.wait()

    def weight(dim, k, back):
        return w_ref[dim, taps - 1 - k if back else k]

    for b in range(2):
        diff = (lax.broadcasted_iota(jnp.int32, band_x.shape[2:], 0)
                - lax.broadcasted_iota(jnp.int32, band_x.shape[2:], 1))
        total = jnp.zeros(diff.shape, F32)
        for k in range(taps):
            total = jnp.where(diff == 128 - rad + k, weight(2, k, b), total)
        hi, lo = split(total)
        band_x[b, 0] = hi
        band_x[b, 1] = lo
        diff = (lax.broadcasted_iota(jnp.int32, (Y, Y + 2 * OFF), 1)
                - lax.broadcasted_iota(jnp.int32, (Y, Y + 2 * OFF), 0))
        total = jnp.zeros(diff.shape, F32)
        for k in range(taps):
            total = jnp.where(diff == OFF - rad + k, weight(1, k, b), total)
        hi, lo = split(total)
        band_y[b] = jnp.concatenate([hi, hi, lo], axis=1)

    def z_pass(pad, back, c):
        ws = [weight(0, k, back) for k in range(taps)]
        nl = cw // 128

        def body(i, _):
            r = pl.ds(pl.multiple_of((i // nl) * 8, 8), 8)
            lane = lax.rem(i, nl) * 128
            src = pl.ds(pl.multiple_of(c * cw + lane, 128), 128)
            dst = pl.ds(pl.multiple_of(lane, 128), 128)
            vals = [pad[p, r, src] for p in range(Z + taps - 1)]
            for z in range(Z):
                t = ws[0] * vals[z]
                for k in range(1, taps):
                    t = t + ws[k] * vals[z + k]
                mid[z, r, dst] = t
            return 0

        lax.fori_loop(0, (Y // 8 + 2) * nl, body, 0)

    G = min(16, Z)

    def y_pass(back, c):
        def body(g, carry):
            rows = []
            for j in range(G):
                hi, lo = split(mid[g * G + j])
                rhs = jnp.concatenate([hi, lo, hi], axis=0)
                rows.append(jnp.dot(band_y[back], rhs, preferred_element_type=F32))
            hi, lo = split(jnp.concatenate(rows, axis=0))
            r = pl.ds(pl.multiple_of(g * G * Y, G * Y), G * Y)
            yh[r, cols(c)] = hi
            yl[r, cols(c)] = lo
            return carry

        lax.fori_loop(0, Z // G, body, 0)

    def x_pass(back, c, use):
        k0, k1 = max(c * cw - 128, 0), min(c * cw + cw + 128, X)
        b0 = k0 - (c * cw - 128)

        def body(g, carry):
            r = pl.ds(pl.multiple_of(g * G * Y, G * Y), G * Y)
            th = band_x[back, 0, b0:b0 + k1 - k0, :]
            tl = band_x[back, 1, b0:b0 + k1 - k0, :]
            h, l = yh[r, k0:k1], yl[r, k0:k1]
            t = (jnp.dot(h, th, preferred_element_type=F32)
                 + jnp.dot(l, th, preferred_element_type=F32)
                 + jnp.dot(h, tl, preferred_element_type=F32))
            use(g, t.reshape(G, Y, cw))
            return carry

        lax.fori_loop(0, Z // G, body, 0)

    def ratio_chunk(c):
        def use(g, t):
            rat_pad[pl.ds(rad + g * G, G), OFF:OFF + Y, cols(c)] = obs[pl.ds(g * G, G), :, cols(c)] / t

        obs_loads[c].wait()
        x_pass(0, c, use)
        start(r_copies[c])

    for c in range(NC):
        est_loads[c].wait()
        wait_send(e_copies[c])
        if c + 1 < NC:
            start(e_copies[c + 1])
        wait_recv(e_copies[c])
        z_pass(est_pad, 0, c)
        y_pass(0, c)
        if c > 0:
            ratio_chunk(c - 1)
    ratio_chunk(NC - 1)

    p_copies = []

    def update_chunk(c):
        mx_all[0, :, cols(c)] = jnp.full((Y, cw), -jnp.inf, F32)

        def use(g, t):
            u = est_pad[pl.ds(rad + g * G, G), OFF:OFF + Y, cols(c)] * t
            out[pl.ds(g * G, G), :, cols(c)] = u
            mx_all[0, :, cols(c)] = jnp.maximum(mx_all[0, :, cols(c)], jnp.max(u, axis=0))

        x_pass(1, c, use)
        for d in range(1, nz):
            i = c * (nz - 1) + d - 1
            copy = pltpu.make_async_remote_copy(
                src_ref=mx_all.at[0, :, cols(c)], dst_ref=mx_all.at[d, :, cols(c)],
                send_sem=p_send.at[i], recv_sem=p_recv.at[i],
                device_id=(lax.rem(gz + d, nz), gy), device_id_type=MESH)
            copy.start()
            p_copies.append(copy)

    for c in range(NC):
        wait_recv(r_copies[c])
        z_pass(rat_pad, 1, c)
        y_pass(1, c)
        if c > 0:
            update_chunk(c - 1)
    update_chunk(NC - 1)

    for copies in r_copies:
        wait_send(copies)
    for copy in p_copies:
        copy.wait_recv()
    best = mx_all[0]
    for d in range(1, nz):
        best = jnp.maximum(best, mx_all[d])
    proj_ref[...] = best
    for copy in p_copies:
        copy.wait_send()


def per_device(nz, ny, observed, estimate, taps_z, taps_y, taps_x):
    Z, Y, X = observed.shape
    taps = taps_z.shape[0]
    rad = (taps - 1) // 2
    pad = (Z + 2 * rad, Y + 16, X)
    cw = 256
    nc = X // cw
    nd = nc * len(DIRS)
    hbm = pl.BlockSpec(memory_space=pltpu.HBM)
    vmem = pl.BlockSpec(memory_space=pltpu.VMEM)
    dma = pltpu.SemaphoreType.DMA
    return pl.pallas_call(
        functools.partial(kernel, nz, ny, cw),
        out_shape=(jax.ShapeDtypeStruct((Z, Y, X), F32), jax.ShapeDtypeStruct((Y, X), F32)),
        in_specs=[hbm] * 5,
        out_specs=(vmem, vmem),
        scratch_shapes=[
            pltpu.VMEM(pad, F32),
            pltpu.VMEM(pad, F32),
            pltpu.VMEM((Z, Y + 16, cw), F32),
            pltpu.VMEM((Z * Y, X), BF16),
            pltpu.VMEM((Z * Y, X), BF16),
            pltpu.VMEM((Z, Y, X), F32),
            pltpu.VMEM((2, 2, cw + 256, cw), BF16),
            pltpu.VMEM((2, Y, 3 * (Y + 16)), BF16),
            pltpu.VMEM((nz, Y, X), F32),
            pltpu.SMEM((3, taps), F32),
            dma((nd,)), dma((nd,)), dma((nd,)), dma((nd,)),
            dma((nc * (nz - 1),)), dma((nc * (nz - 1),)), dma((2 * nc,)), dma((3,)),
        ],
        compiler_params=pltpu.CompilerParams(
            collective_id=0, has_side_effects=True, vmem_limit_bytes=50 * 1024 * 1024),
        name="deconvolve",
    )(observed, estimate, taps_z, taps_y, taps_x)


def solution(mesh):
    return jax.shard_map(
        functools.partial(per_device, mesh.shape["gz"], mesh.shape["gy"]),
        mesh=mesh,
        in_specs=(P("gz", "gy", None), P("gz", "gy", None), P(), P(), P()),
        out_specs=(P("gz", "gy", None), P("gy", None)),
        check_vma=False,
    )
```

time: 54.4 us -> 42.2 us (0.78)
  the two profiles are of different devices: /device:TPU:20 before, /device:TPU:9 now
where the time goes in v2:
time: 42.2 us; the launch traced here: 42 us
  Pallas kernels  37.1 us (88%)
  local copies, waits for them, and re-layouts  4.26 us (10%)
  between operations  0.65 us (2%)
    pallas_call x1, Pallas kernels, per_device(): pl.pallas_call(functools.partial(kernel, nz, ny, cw), out_shape=(jax.Shap...  37.1 us
    unnamed x8, local copies, waits for them, and re-layouts  4.26 us

profile of v2, /device:TPU:9, one launch (start us, length us, event | category | flops | bytes accessed | tf_op | source)
XLA Modules:
  0.0 42.0 jit_solution(9564571351464737998)
XLA Ops:
  0.6 0.0 copy-start
  0.6 0.6 %copy-done = f32[9]{0:T(128)S(1)} copy-done((f32[9]{0:T(128)S(1)}, f32[9]{0:T(128)}, u32[]{:S(2)}) %copy-start) | copy-done | bytes 60
  1.3 0.0 copy-start.1
  1.3 0.7 %copy-done.1 = f32[9]{0:T(128)S(1)} copy-done((f32[9]{0:T(128)S(1)}, f32[9]{0:T(128)}, u32[]{:S(2)}) %copy-start.1) | copy-done | bytes 60
  1.9 0.0 copy-start.2
  1.9 0.7 %copy-done.2 = f32[9]{0:T(128)S(1)} copy-done((f32[9]{0:T(128)S(1)}, f32[9]{0:T(128)}, u32[]{:S(2)}) %copy-start.2) | copy-done | bytes 60
  2.6 37.1 %deconvolve.1 = (f32[32,32,768]{2,1,0:T(8,128)S(1)}, f32[32,768]{1,0:T(8,128)S(1)}) custom-call(f32[32,32,768]{2,1,0:T(8,128)} %obs_hbm.1, f32[32,32,768]{2,1,0:T(8,128)} %est_hbm.1, f32[9]{0:T(128)S(1)} %copy-done, f32[9]{0:T(128)S(1)} %copy-done.1, f32[9]{0:T(128)S(1)} %copy-done.2), custom_call_target="tpu_custom_call" | custom-call | tf_op jit(solution)/shard_map/deconvolve/pallas_call | solution.py:271
  39.7 1.7 %copy.9 = f32[32,32,768]{2,1,0:T(8,128)} copy(f32[32,32,768]{2,1,0:T(8,128)S(1)} %get-tuple-element.4) | data formatting | bytes 6291456
  41.3 0.6 %copy.10 = f32[32,768]{1,0:T(8,128)} copy(f32[32,768]{1,0:T(8,128)S(1)} %get-tuple-element.5) | data formatting | bytes 196608
Async XLA Ops:
  0.6 0.7 %copy-start = (f32[9]{0:T(128)S(1)}, f32[9]{0:T(128)}, u32[]{:S(2)}) copy-start(f32[9]{0:T(128)} %wz_hbm.1) | copy-start | bytes 112
  1.3 0.7 %copy-start.1 = (f32[9]{0:T(128)S(1)}, f32[9]{0:T(128)}, u32[]{:S(2)}) copy-start(f32[9]{0:T(128)} %wy_hbm.1) | copy-start | bytes 112
  1.9 0.7 %copy-start.2 = (f32[9]{0:T(128)S(1)}, f32[9]{0:T(128)}, u32[]{:S(2)}) copy-start(f32[9]{0:T(128)} %wx_hbm.1) | copy-start | bytes 112
